TPU v7x, 128 devices: a whole 4x4x4 slice. The times are simulated.
128 devices in a mesh: dp: 16 (over y_hi, x, core), tensor: 8 (over z, y_lo).
Axes of the slice: x: 4, y: 4 (y_hi: 2, y_lo: 2; y = y_hi * 2 + y_lo), z: 4, core: 2. Of those that a mesh axis runs over, the one named last changes fastest.
Arguments:
- out_grad: bfloat16 [8192, 4096], P(('dp', 'tensor')), may hold values from -24 to 24
- hidden_act: bfloat16 [8192, 14336], P('dp', 'tensor'), may hold values from -6 to 6
- w_down: bfloat16 [4096, 14336], P(None, 'tensor'), may hold values from -0.09375 to 0.09375
Outputs:
- hidden_grad: bfloat16 [8192, 14336], P('dp', 'tensor')
- weight_grad: bfloat16 [4096, 14336], P('dp', 'tensor')
- factor: float32 [4096, 4096], P('dp', 'tensor')
All inputs are finite; a program needn't handle non-finite values.
Results may differ from a plain program's by a relative error of at most 0.02.
Values may be sent and summed in bfloat16 or wider, within the bound.
A program may use at most 128 MiB of HBM per device.

v0:
```python
import math

import jax
import jax.numpy as jnp
from jax import lax
from jax.sharding import PartitionSpec as P


def contract_rows(left, right):
    return lax.dot_general(
        left, right, (((0,), (0,)), ((), ())), preferred_element_type=jnp.float32
    )


def shards(out_grad, hidden_act, w_down):
    groups = lax.axis_size("dp")
    width = w_down.shape[0]
    block = width // lax.axis_size("tensor")
    column = lax.axis_index("tensor")
    share = width // groups
    total = out_grad.shape[0] * lax.axis_size("tensor") * groups
    scale = 1.0 / math.sqrt(total)
    gathered = lax.all_gather(out_grad, "tensor", axis=0, tiled=True)
    hidden_grad = jnp.dot(gathered, w_down, preferred_element_type=jnp.float32).astype(jnp.bfloat16)
    own_cols = lax.dynamic_slice_in_dim(gathered, column * block, block, 1)
    factor_term = contract_rows(gathered, own_cols) / total
    weight_grad = lax.psum_scatter(
        (contract_rows(gathered, hidden_act) * scale).astype(jnp.bfloat16),
        "dp",
        scatter_dimension=0,
        tiled=True,
    )
    summed = lax.psum(factor_term.astype(jnp.bfloat16), "dp").astype(jnp.float32)
    factor = lax.dynamic_slice_in_dim(summed, lax.axis_index("dp") * share, share, 0)
    return (hidden_grad, weight_grad, factor)


def solution(mesh):
    placed = (P(("dp", "tensor"), None), P("dp", "tensor"), P(None, "tensor"))
    return jax.shard_map(
        shards,
        mesh=mesh,
        in_specs=placed,
        out_specs=(P("dp", "tensor"), P("dp", "tensor"), P("dp", "tensor")),
        check_vma=False,
    )
```

profile of v0, /device:TPU:1, one launch (start us, length us, event | category | flops | bytes accessed | tf_op | source)
XLA Modules:
  0.0 404.9 jit_solution(228321215761123057)
XLA Ops:
  7.2 0.0 copy-start
  7.2 0.0 all-gather.2.cloned.1.call-start
  7.2 0.7 all-gather.2.cloned.1.call-update
  7.9 0.0 all-reduce.2.cloned.1.call-start
  8.0 95.7 %all-gather.2.cloned.1.call-done = bf16[512,4096]{1,0:T(8,128)(2,1)} async-done(((bf16[64,4096]{1,0:T(8,128)(2,1)}), bf16[512,4096]{1,0:T(8,128)(2,1)}) %all-gather.2.cloned.1.call-update) | async-done | bytes 4194320 | tf_op jit(solution)/shard_map/all_gather | solution.py:23
  103.6 6.7 %fusion = bf16[4096,512]{0,1:T(8,128)(2,1)} fusion(bf16[512,4096]{1,0:T(8,128)(2,1)} %all-gather.2.cloned.1.call-done, s32[]{:T(128)S(6)} %select_n.6), kind=kOutput, calls=%fused_computation.2 | convolution fusion | flops 2151677952 | bytes 8912900 | tf_op jit(solution)/shard_map/dot_general | solution.py:10
  110.4 0.0 all-reduce.2.cloned.1.call-update
  110.4 0.0 reduce-scatter.2.cloned.1.call-start
  110.5 0.0 copy-done
  110.5 14.4 %multiply_convert_fusion = bf16[4096,1792]{1,0:T(8,128)(2,1)} fusion(bf16[512,4096]{1,0:T(8,128)(2,1)} %all-gather.2.cloned.1.call-done, bf16[512,1792]{1,0:T(8,128)(2,1)S(1)} %copy-done), kind=kOutput, calls=%fused_computation | convolution fusion | flops 7530872832 | bytes 20709376 | tf_op jit(solution)/shard_map/dot_general | solution.py:10
  124.9 0.0 reduce-scatter.2.cloned.1.call-update
  124.9 14.3 %convolution_convert_fusion = bf16[512,1792]{1,0:T(8,128)(2,1)} fusion(bf16[512,4096]{1,0:T(8,128)(2,1)} %all-gather.2.cloned.1.call-done, bf16[4096,1792]{1,0:T(8,128)(2,1)} %param.5), kind=kOutput, calls=%fused_computation.3 | convolution fusion | flops 7517110272 | bytes 20709376 | tf_op jit(solution)/shard_map/dot_general | solution.py:24
  139.2 121.0 %all-reduce.2.cloned.1.call-done = bf16[4096,512]{0,1:T(8,128)(2,1)} async-done(((bf16[4096,512]{0,1:T(8,128)(2,1)}), bf16[4096,512]{0,1:T(8,128)(2,1)}) %all-reduce.2.cloned.1.call-update) | async-done | bytes 4194320 | tf_op jit(solution)/shard_map/psum | solution.py:33
  260.2 1.0 dynamic-slice_convert_fusion
  261.2 1.0 copy.6
  262.2 136.2 %reduce-scatter.2.cloned.1.call-done = bf16[256,1792]{1,0:T(8,128)(2,1)} async-done(((bf16[4096,1792]{1,0:T(8,128)(2,1)}), bf16[256,1792]{1,0:T(8,128)(2,1)}) %reduce-scatter.2.cloned.1.call-update) | async-done | bytes 917520 | tf_op jit(solution)/shard_map/reduce_scatter | solution.py:27
Async XLA Ops:
  7.2 103.3 %copy-start = (bf16[512,1792]{1,0:T(8,128)(2,1)S(1)}, bf16[512,1792]{1,0:T(8,128)(2,1)}, u32[]{:S(2)}) copy-start(bf16[512,1792]{1,0:T(8,128)(2,1)} %param.4) | copy-start | bytes 5505028
  7.2 96.5 %all-gather.2.cloned.1.call-start = ((), (), s32[]{:S(2)}) async-start(), calls=%async_computation.1 | async-start | bytes 4718592 | tf_op jit(solution)/shard_map/all_gather | solution.py:23
  7.9 252.3 %all-reduce.2.cloned.1.call-start = ((), (), s32[]{:S(2)}) async-start(), calls=%async_computation.3 | async-start | bytes 8388608 | tf_op jit(solution)/shard_map/psum | solution.py:33
  110.4 288.0 %reduce-scatter.2.cloned.1.call-start = ((), (), s32[]{:S(2)}) async-start(), calls=%async_computation.2 | async-start | bytes 15597568 | tf_op jit(solution)/shard_map/reduce_scatter | solution.py:27
Sparse Core Ops, SparseCore 0:
  9.7 93.9 all-gather.1
  110.5 149.6 all-reduce.1
  265.2 133.2 reduce-scatter.1
where the time goes:
time: 405 us
  waiting for transfers between devices  354 us (87%)
  matrix products  35.4 us (9%)
  between operations  13.8 us (3%)
    reduce_scatter x1, waiting for transfers between devices, shards(): lax.psum_scatter((contract_rows(gathered, hidden_act) * scale).astype(jnp...  136 us
    psum x1, waiting for transfers between devices, shards(): lax.psum(factor_term.astype(jnp.bfloat16), 'dp').astype(jnp.float32)  121 us
    all_gather x1, waiting for transfers between devices, shards(): gathered = lax.all_gather(out_grad, 'tensor', axis=0, tiled=True)  95.7 us
    dot_general x2, matrix products, contract_rows(): lax.dot_general(left, right, (((0,), (0,)), ((), ())), preferred_element_...  21.1 us
    dot_general x1, matrix products, shards(): jnp.dot(gathered, w_down, preferred_element_type=jnp.float32)  14.3 us
  transfers between devices with their start and end apart: 3, of which 3 were waited for; matrix products, arithmetic and copies ran while one was open for 8% of the time, Pallas kernels for 0%

commit v1 on v0

v1 whole, which is shorter than its diff:
```python
import math

import jax
import jax.numpy as jnp
from jax import lax
from jax.experimental import pallas as pl
from jax.experimental.pallas import tpu as pltpu
from jax.sharding import PartitionSpec as P

MESH = pl.DeviceIdType.MESH
BF16 = jnp.bfloat16
F32 = jnp.float32

ORDER = ((1, 2), (1, 1), (1, 3), (0, 2), (0, 1), (0, 3), (1, 0), (0, 0))
SLOT = {pair: slot for slot, pair in enumerate(ORDER)}
CHIPS = len(ORDER)
TILE = 256
FIRST_X = 1024
COPIES = 96


def kernel(own_grad, own_act, weight, hidden_out, wgrad_out, factor_out,
           grad, grad_sib, grad_cols, act, w, left, part_w, part_f, hidden, wgrad, factor, boxes, send_sem, recv_sem, local_sem):
    rows, width = own_grad.shape
    tokens, units = own_act.shape
    tensor = tokens // rows
    chunk = width // CHIPS
    share = chunk // 2
    half = share // 2
    dp, t = lax.axis_index("dp"), lax.axis_index("tensor")
    core, x, y = dp % 2, (dp // 2) % 4, dp // 8
    z, y_lo = t // 2, t % 2

    def on_x(step):
        return (y * 8 + ((x + step) % 4) * 2 + core, t)

    def on_z(step):
        return (dp, ((z + step) % 4) * 2 + y_lo)

    sibling = (dp + 1 - 2 * core, t)
    right, left_chip = on_x(1), on_x(3)
    across = ((1 - y) * 8 + x * 2 + core, t)
    partner = (dp, z * 2 + 1 - y_lo)
    near_z = (on_z(1), on_z(3), on_z(2))

    barrier = pltpu.get_barrier_semaphore()
    everyone = (sibling, right, left_chip, across, partner) + near_z
    for device in everyone:
        pl.semaphore_signal(barrier, inc=1, device_id=device, device_id_type=MESH)

    remotes, locals_ = [], []

    def send(src, dst, device):
        number = len(remotes)
        copy = pltpu.make_async_remote_copy(
            src_ref=src, dst_ref=dst, send_sem=send_sem.at[number], recv_sem=recv_sem.at[number],
            device_id=device, device_id_type=MESH)
        copy.start()
        remotes.append(copy)
        return copy

    def move(src, dst):
        copy = pltpu.make_async_copy(src, dst, local_sem.at[len(locals_)])
        copy.start()
        locals_.append(copy)
        return copy

    def first_col(slot):
        dy, dx = ORDER[slot]
        return (((y + dy) % 2) * 4 + (x + dx) % 4) * chunk

    def columns(slot):
        return pl.ds(pl.multiple_of(first_col(slot), chunk), chunk)

    def share_of(slot, which):
        return pl.ds(pl.multiple_of(first_col(slot) + which * share, share), share)

    own_rows = pl.ds(pl.multiple_of(t * rows, rows), rows)
    pair_rows = pl.ds(pl.multiple_of(z * 2 * rows, 2 * rows), 2 * rows)

    own_here = move(own_grad, grad.at[own_rows, :])
    act_here = move(own_act, act.at[pl.ds(0, tokens)])
    pl.semaphore_wait(barrier, len(everyone))

    from_partner = [send(own_grad.at[:, columns(s)], grad.at[own_rows, columns(s)], partner) for s in range(CHIPS)]
    act_there = send(own_act, act.at[pl.ds(tokens, tokens)], sibling)
    w_here = move(weight, w)
    along_z, to_sibling = {}, {}

    def gather_z(slot):
        from_partner[slot].wait_recv()
        piece = grad.at[pair_rows, columns(slot)]
        along_z[slot] = [send(piece, piece, device) for device in near_z]

    def gather_sibling(slot):
        for copy in along_z[slot]:
            copy.wait_recv()
        to_sibling[slot] = send(grad.at[:, share_of(slot, 1 - core)], grad_sib.at[slot], sibling)

    class Columns:
        def __init__(self, part, start, count, x_first, box):
            self.part, self.cols, self.x_first = part, pl.ds(start, count), x_first
            self.relay_l, self.relay_r, self.end_l, self.end_r, self.box_y = box
            self.relays, self.ends, self.over_y = {}, {}, {}

        def at(self, dy, dx, low=0, count=share):
            return self.part.at[SLOT[dy, dx], pl.ds(low, count), self.cols]

        def far(self, dy):
            self.relays[dy] = (
                send(self.at(dy, 2, 0, half), self.relay_l.at[dy], right),
                send(self.at(dy, 2, half, half), self.relay_r.at[dy], left_chip))

        def near_right(self, dy):
            self.ends[dy, 1, 1] = send(self.at(dy, 1, half, half), self.end_l.at[dy, pl.ds(half, half)], right)

        def near_left(self, dy):
            self.ends[dy, 3, 0] = send(self.at(dy, 3, 0, half), self.end_r.at[dy, pl.ds(0, half)], left_chip)

        def relay_right(self, dy):
            self.relays[dy][0].wait_recv()
            mine = self.at(dy, 1, 0, half)
            mine[...] = (mine[...].astype(F32) + self.relay_l[dy].astype(F32)).astype(BF16)
            self.ends[dy, 1, 0] = send(mine, self.end_l.at[dy, pl.ds(0, half)], right)

        def relay_left(self, dy):
            self.relays[dy][1].wait_recv()
            mine = self.at(dy, 3, half, half)
            mine[...] = (mine[...].astype(F32) + self.relay_r[dy].astype(F32)).astype(BF16)
            self.ends[dy, 3, 1] = send(mine, self.end_r.at[dy, pl.ds(half, half)], left_chip)

        def x_sum(self, dy):
            for place in ((1, 0), (1, 1), (3, 0), (3, 1)):
                self.ends[(dy,) + place].wait_recv()
            return self.at(dy, 0)[...].astype(F32) + self.end_l[dy].astype(F32) + self.end_r[dy].astype(F32)

        def send_y(self, dx):
            self.over_y[dx] = send(self.at(1, dx), self.box_y.at[dx], across)

        def add_y(self, dx):
            self.over_y[dx].wait_recv()
            mine = self.at(0, dx)
            mine[...] = (mine[...].astype(F32) + self.box_y[dx].astype(F32)).astype(BF16)

        def end_y(self):
            self.at(1, 0)[...] = self.x_sum(1).astype(BF16)
            self.over_y[0] = send(self.at(1, 0), self.box_y, across)

        def total(self):
            value = self.x_sum(0)
            if self.x_first:
                self.over_y[0].wait_recv()
                value = value + self.box_y[...].astype(F32)
            return value

    wx = Columns(part_w, 0, FIRST_X, True, boxes[0:5])
    wy = Columns(part_w, FIRST_X, units - FIRST_X, False, boxes[5:10])
    fx = Columns(part_f, 0, chunk, True, boxes[10:15])

    def multiply(slot):
        to_sibling[slot].wait_recv()
        left[slot, :, pl.ds(0, tokens)] = grad[:, share_of(slot, core)].T
        left[slot, :, pl.ds(tokens, tokens)] = grad_sib[slot].T

        @pl.loop(0, units // TILE)
        def _(n):
            cols = pl.ds(pl.multiple_of(n * TILE, TILE), TILE)
            part_w[slot, :, cols] = jnp.dot(left[slot], act[:, cols], preferred_element_type=F32).astype(BF16)

    def multiply_factor(slot):
        own = left[slot, :, pl.ds(0, tokens)]
        other = left[slot, :, pl.ds(tokens, tokens)]
        cols = pl.ds(pl.multiple_of(t * chunk, chunk), chunk)
        value = jnp.dot(own, grad[:, cols], preferred_element_type=F32)
        value = value + jnp.dot(other, grad_cols[...], preferred_element_type=F32)
        part_f[slot] = value.astype(BF16)

    def multiply_hidden(first, last):
        @pl.loop(first, last)
        def _(n):
            cols = pl.ds(pl.multiple_of(n * TILE, TILE), TILE)
            hidden[:, cols] = jnp.dot(grad[...], w[:, cols], preferred_element_type=F32).astype(BF16)

    own_here.wait()
    gather_z(0)
    gather_z(1)
    gather_sibling(0)
    act_here.wait()
    act_there.wait_recv()
    for slot, (dy, dx) in enumerate(ORDER):
        multiply(slot)
        if dx == 2:
            wx.far(dy)
        if dx == 1:
            wx.near_right(dy)
        if dx == 3:
            wx.near_left(dy)
        if dy == 1:
            wy.send_y(dx)
        if slot + 2 < CHIPS:
            gather_z(slot + 2)
        if dx == 1:
            wx.relay_right(dy)
        if dx == 3:
            wx.relay_left(dy)
        if slot + 1 < CHIPS:
            gather_sibling(slot + 1)
        else:
            cols = pl.ds(pl.multiple_of(t * chunk, chunk), chunk)
            to_sibling["cols"] = send(grad.at[:, cols], grad_cols, sibling)
        if dy == 0 and dx != 0:
            wy.add_y(dx)
            if dx == 2:
                wy.far(0)
            if dx == 1:
                wy.near_right(0)
                wy.relay_right(0)
            if dx == 3:
                wy.near_left(0)
                wy.relay_left(0)

    to_sibling["cols"].wait_recv()
    for slot, (dy, dx) in enumerate(ORDER):
        multiply_factor(slot)
        if dx == 2:
            fx.far(dy)
        if dx == 1:
            fx.near_right(dy)
        if dx == 3:
            fx.near_left(dy)
    wx.end_y()
    w_here.wait()
    multiply_hidden(0, 2)
    for dy in (1, 0):
        fx.relay_right(dy)
        fx.relay_left(dy)
    multiply_hidden(2, 5)
    fx.end_y()
    multiply_hidden(5, units // TILE)
    hidden_done = move(hidden, hidden_out)

    scale = 1.0 / math.sqrt(tokens * 16)
    wy.add_y(0)
    wgrad[:, wx.cols] = (wx.total() * scale).astype(BF16)
    wgrad[:, wy.cols] = (wy.total() * scale).astype(BF16)
    wgrad_done = move(wgrad, wgrad_out)
    factor[...] = fx.total() / (tokens * 16)
    factor_done = move(factor, factor_out)
    for copy in remotes:
        copy.wait_send()
    for copy in (hidden_done, wgrad_done, factor_done):
        copy.wait()


def shards(out_grad, hidden_act, w_down):
    rows, width = out_grad.shape
    tokens, units = hidden_act.shape
    chunk = width // CHIPS
    share, half = chunk // 2, chunk // 4

    def boxes(count, x_first):
        ways = 2 if x_first else 1
        relay, end = pltpu.VMEM((ways, half, count), BF16), pltpu.VMEM((ways, share, count), BF16)
        over = pltpu.VMEM((share, count) if x_first else (4, share, count), BF16)
        return [relay, relay, end, end, over]

    def body(*refs):
        kernel(*refs[:17], refs[17:32], *refs[32:])

    return pl.pallas_call(
        body,
        out_shape=(
            jax.ShapeDtypeStruct((tokens, units), BF16),
            jax.ShapeDtypeStruct((share, units), BF16),
            jax.ShapeDtypeStruct((share, chunk), F32),
        ),
        in_specs=[pl.BlockSpec(memory_space=pl.ANY)] * 3,
        out_specs=(pl.BlockSpec(memory_space=pl.ANY),) * 3,
        scratch_shapes=[
            pltpu.VMEM((tokens, width), BF16),
            pltpu.VMEM((CHIPS, tokens, share), BF16),
            pltpu.VMEM((tokens, chunk), BF16),
            pltpu.VMEM((2 * tokens, units), BF16),
            pltpu.VMEM((width, units), BF16),
            pltpu.VMEM((CHIPS, share, 2 * tokens), BF16),
            pltpu.VMEM((CHIPS, share, units), BF16),
            pltpu.VMEM((CHIPS, share, chunk), BF16),
            pltpu.VMEM((tokens, units), BF16),
            pltpu.VMEM((share, units), BF16),
            pltpu.VMEM((share, chunk), F32),
            *boxes(FIRST_X, True),
            *boxes(units - FIRST_X, False),
            *boxes(chunk, True),
            pltpu.SemaphoreType.DMA((COPIES,)),
            pltpu.SemaphoreType.DMA((COPIES,)),
            pltpu.SemaphoreType.DMA((8,)),
        ],
        compiler_params=pltpu.CompilerParams(
            collective_id=0, has_side_effects=True, vmem_limit_bytes=60 * 2**20),
    )(out_grad, hidden_act, w_down)


def solution(mesh):
    return jax.shard_map(
        shards,
        mesh=mesh,
        in_specs=(P(("dp", "tensor"), None), P("dp", "tensor"), P(None, "tensor")),
        out_specs=(P("dp", "tensor"), P("dp", "tensor"), P("dp", "tensor")),
        check_vma=False,
    )
```

time: 405 us -> 107 us (0.26)
  waiting for transfers between devices: 354 us -> 0 us
  Pallas kernels: 0 us -> 99.1 us
  matrix products: 35.4 us -> 0 us
  between operations: 13.8 us -> 0.65 us
  local copies, waits for them, and re-layouts: 1.01 us -> 5.09 us
    reduce_scatter x1 -> x0, waiting for transfers between devices: 136 us -> none  [shards(): lax.psum_scatter((contract_rows(gathered, hidden_act) * scale).astype(jnp...]
    psum x1 -> x0, waiting for transfers between devices: 121 us -> none  [shards(): lax.psum(factor_term.astype(jnp.bfloat16), 'dp').astype(jnp.float32)]
    pallas_call x0 -> x1, Pallas kernels: none -> 99.1 us  [shards(): pl.pallas_call(body, out_shape=(jax.ShapeDtypeStruct((tokens, units), BF1...]
    all_gather x1 -> x0, waiting for transfers between devices: 95.7 us -> none  [shards(): gathered = lax.all_gather(out_grad, 'tensor', axis=0, tiled=True)]
    dot_general x3 -> x0, matrix products: 35.4 us -> none  [the longest x2 21.1 us: contract_rows(): lax.dot_general(left, right, (((0,), (0,)), ((), ())), preferred_element_...]
    unnamed x3 -> x7, local copies, waits for them, and re-layouts: 1.01 us -> 5.09 us
  transfers between devices with their start and end apart: 3 -> 0, of which waited for: 3 -> 0; matrix products, arithmetic and copies ran while one was open for 8% -> 0% of each run, Pallas kernels for 0% -> 0%
where the time goes in v1:
time: 107 us; the launch traced here: 105 us
  Pallas kernels  99.1 us (93%)
  local copies, waits for them, and re-layouts  5.09 us (5%)
    pallas_call x1, Pallas kernels, shards(): pl.pallas_call(body, out_shape=(jax.ShapeDtypeStruct((tokens, units), BF1...  99.1 us
    unnamed x7, local copies, waits for them, and re-layouts  5.09 us

profile of v1, /device:TPU:1, one launch (start us, length us, event | category | flops | bytes accessed | tf_op | source)
XLA Modules:
  0.0 104.9 jit_solution(9073430803687934921)
XLA Ops:
  0.6 99.1 %shard_map.58 = (bf16[512,1792]{1,0:T(8,128)(2,1)}, bf16[256,1792]{1,0:T(8,128)(2,1)}, f32[256,512]{1,0:T(8,128)}) custom-call(bf16[64,4096]{1,0:T(8,128)(2,1)} %refs_0_.1, bf16[512,1792]{1,0:T(8,128)(2,1)} %refs_1_.1, bf16[4096,1792]{1,0:T(8,128)(2,1)} %refs_2_.1), custom_call_target="tpu_custom_call" | custom-call | tf_op jit(solution)/shard_map/pallas_call | solution.py:270
  99.8 0.0 copy-start
  99.8 2.9 %copy.9 = bf16[512,1792]{1,0:T(8,128)(2,1)} copy(bf16[512,1792]{1,0:T(8,128)(2,1)} %get-tuple-element.6) | data formatting | bytes 3670016
  102.7 0.0 copy-done
  102.7 0.0 copy-start.1
  102.7 0.9 copy.10
  103.6 0.4 copy-done.1
  104.1 0.8 copy.11
Async XLA Ops:
  99.8 2.9 %copy-start = (bf16[256,1792]{1,0:T(8,128)(2,1)S(1)}, bf16[256,1792]{1,0:T(8,128)(2,1)}, u32[]{:S(2)}) copy-start(bf16[256,1792]{1,0:T(8,128)(2,1)} %get-tuple-element.7) | copy-start | bytes 2752516
  102.7 1.4 %copy-start.1 = (f32[256,512]{1,0:T(8,128)S(1)}, f32[256,512]{1,0:T(8,128)}, u32[]{:S(2)}) copy-start(f32[256,512]{1,0:T(8,128)} %get-tuple-element.8) | copy-start | bytes 1572868

commit v2 on v1

--- a/solution.py
+++ b/solution.py
@@ -11,19 +11,34 @@
 BF16 = jnp.bfloat16
 F32 = jnp.float32
 
-ORDER = ((1, 2), (1, 1), (1, 3), (0, 2), (0, 1), (0, 3), (1, 0), (0, 0))
+ORDER = ((1, 2), (0, 2), (1, 1), (1, 3), (0, 3), (0, 1), (1, 0), (0, 0))
 SLOT = {pair: slot for slot, pair in enumerate(ORDER)}
 CHIPS = len(ORDER)
 TILE = 256
-FIRST_X = 1024
-COPIES = 96
+FIRST_X = 896
+COPIES = 128
+
+
+EARLY = (0,)
+PLAN = (
+    ("z", 0), ("z", 1), ("z", 2), ("z", 3), ("z", 4), ("sib", 0), ("mul", 0), ("x", "w", 0), ("y", 2), ("z", 5),
+    ("sib", 1), ("mul", 1), ("x", "w", 1), ("sib", 2), ("mul", 2), ("x", "w", 2), ("relay", "w", 2), ("y", 1),
+    ("z", 6), ("addy", 2), ("x", "v", 1), ("sib", 3), ("mul", 3), ("relay", "w", 3), ("y", 3), ("sib", 4), ("mul", 4),
+    ("relay", "w", 4), ("x", "w", 3), ("z", 7), ("cols",), ("sib", 5), ("mul", 5), ("addy", 1), ("relay", "v", 5),
+    ("relay", "w", 5), ("x", "w", 5), ("addy", 3), ("relay", "v", 4), ("x", "v", 4), ("sib", 7), ("sib", 6),
+    ("hid", 0, 1), ("mul", 6), ("y", 0), ("endy", "w"), ("colsib",), ("fac", 0), ("fac", 6), ("fac", 2), ("fac", 1),
+    ("x", "f", 0), ("fac", 5), ("fac", 4), ("x", "f", 5), ("fac", 3), ("x", "f", 3), ("relay", "f", 2),
+    ("relay", "f", 3), ("x", "f", 2), ("x", "f", 1), ("x", "f", 4), ("x", "w", 4), ("x", "v", 5), ("hid", 1, 5),
+    ("relay", "f", 4), ("endy", "f"), ("hid", 5, 7), ("relay", "f", 5), ("mul", 7), ("fac", 7), ("addy", 0),
+    ("fin", "v"), ("fin", "w"), ("fin", "f"),
+)
 
 
 def kernel(own_grad, own_act, weight, hidden_out, wgrad_out, factor_out,
-           grad, grad_sib, grad_cols, act, w, left, part_w, part_f, hidden, wgrad, factor, boxes, send_sem, recv_sem, local_sem):
+           grad, grad_sib, cols_own, cols_sib, act, w, left, part_w, part_f, hidden, wgrad, factor, boxes,
+           send_sem, recv_sem, local_sem, w_sem):
     rows, width = own_grad.shape
     tokens, units = own_act.shape
-    tensor = tokens // rows
     chunk = width // CHIPS
     share = chunk // 2
     half = share // 2
@@ -41,10 +56,10 @@
     right, left_chip = on_x(1), on_x(3)
     across = ((1 - y) * 8 + x * 2 + core, t)
     partner = (dp, z * 2 + 1 - y_lo)
-    near_z = (on_z(1), on_z(3), on_z(2))
+    along = (2, 1, 3)
 
     barrier = pltpu.get_barrier_semaphore()
-    everyone = (sibling, right, left_chip, across, partner) + near_z
+    everyone = (sibling, right, left_chip, across, partner) + tuple(on_z(step) for step in along)
     for device in everyone:
         pl.semaphore_signal(barrier, inc=1, device_id=device, device_id_type=MESH)
 
@@ -75,27 +90,52 @@
     def share_of(slot, which):
         return pl.ds(pl.multiple_of(first_col(slot) + which * share, share), share)
 
+    def columns_of(there):
+        return pl.ds(pl.multiple_of(there * chunk, chunk), chunk)
+
     own_rows = pl.ds(pl.multiple_of(t * rows, rows), rows)
+    partner_rows = pl.ds(pl.multiple_of((z * 2 + 1 - y_lo) * rows, rows), rows)
     pair_rows = pl.ds(pl.multiple_of(z * 2 * rows, 2 * rows), 2 * rows)
+
+    def w_tile(n):
+        cols = pl.ds(pl.multiple_of(n * TILE, TILE), TILE)
+        return pltpu.make_async_copy(weight.at[:, cols], w.at[n % 2], w_sem.at[n % 2])
 
     own_here = move(own_grad, grad.at[own_rows, :])
     act_here = move(own_act, act.at[pl.ds(0, tokens)])
     pl.semaphore_wait(barrier, len(everyone))
 
-    from_partner = [send(own_grad.at[:, columns(s)], grad.at[own_rows, columns(s)], partner) for s in range(CHIPS)]
-    act_there = send(own_act, act.at[pl.ds(tokens, tokens)], sibling)
-    w_here = move(weight, w)
-    along_z, to_sibling = {}, {}
+    from_partner, along_z, to_sibling, cols = {}, {}, {}, {}
+
+    def gather_y(slot):
+        piece = columns(slot)
+        from_partner[slot] = send(own_grad.at[:, piece], grad.at[own_rows, piece], partner)
+
+    def gather_own(slot):
+        piece = columns(slot)
+        along_z[slot] = [send(own_grad.at[:, piece], grad.at[own_rows, piece], on_z(step)) for step in along]
 
     def gather_z(slot):
         from_partner[slot].wait_recv()
-        piece = grad.at[pair_rows, columns(slot)]
-        along_z[slot] = [send(piece, piece, device) for device in near_z]
+        piece = grad.at[partner_rows if slot in EARLY else pair_rows, columns(slot)]
+        along_z.setdefault(slot, []).extend([send(piece, piece, on_z(step)) for step in along])
 
     def gather_sibling(slot):
         for copy in along_z[slot]:
             copy.wait_recv()
         to_sibling[slot] = send(grad.at[:, share_of(slot, 1 - core)], grad_sib.at[slot], sibling)
+
+    def cols_z():
+        cols["here"] = move(grad.at[pair_rows, columns_of(t)], cols_own.at[pair_rows, :])
+        cols["z"] = [
+            send(grad.at[pair_rows, columns_of(((z + step) % 4) * 2 + y_lo)], cols_own.at[pair_rows, :], on_z(step))
+            for step in along]
+
+    def cols_sibling():
+        cols["here"].wait()
+        for copy in cols["z"]:
+            copy.wait_recv()
+        cols["sibling"] = send(cols_own, cols_sib, sibling)
 
     class Columns:
         def __init__(self, part, start, count, x_first, box):
@@ -157,6 +197,8 @@
     wy = Columns(part_w, FIRST_X, units - FIRST_X, False, boxes[5:10])
     fx = Columns(part_f, 0, chunk, True, boxes[10:15])
 
+    sets = {"w": wx, "v": wy, "f": fx}
+
     def multiply(slot):
         to_sibling[slot].wait_recv()
         left[slot, :, pl.ds(0, tokens)] = grad[:, share_of(slot, core)].T
@@ -164,87 +206,65 @@
 
         @pl.loop(0, units // TILE)
         def _(n):
-            cols = pl.ds(pl.multiple_of(n * TILE, TILE), TILE)
-            part_w[slot, :, cols] = jnp.dot(left[slot], act[:, cols], preferred_element_type=F32).astype(BF16)
+            tile = pl.ds(pl.multiple_of(n * TILE, TILE), TILE)
+            part_w[slot, :, tile] = jnp.dot(left[slot], act[:, tile], preferred_element_type=F32).astype(BF16)
 
     def multiply_factor(slot):
-        own = left[slot, :, pl.ds(0, tokens)]
-        other = left[slot, :, pl.ds(tokens, tokens)]
-        cols = pl.ds(pl.multiple_of(t * chunk, chunk), chunk)
-        value = jnp.dot(own, grad[:, cols], preferred_element_type=F32)
-        value = value + jnp.dot(other, grad_cols[...], preferred_element_type=F32)
+        if slot == 0:
+            cols["sibling"].wait_recv()
+        value = jnp.dot(left[slot, :, pl.ds(0, tokens)], cols_own[...], preferred_element_type=F32)
+        value = value + jnp.dot(left[slot, :, pl.ds(tokens, tokens)], cols_sib[...], preferred_element_type=F32)
         part_f[slot] = value.astype(BF16)
 
     def multiply_hidden(first, last):
         @pl.loop(first, last)
         def _(n):
-            cols = pl.ds(pl.multiple_of(n * TILE, TILE), TILE)
-            hidden[:, cols] = jnp.dot(grad[...], w[:, cols], preferred_element_type=F32).astype(BF16)
-
+            w_tile(n).wait()
+            tile = pl.ds(pl.multiple_of(n * TILE, TILE), TILE)
+            hidden[:, tile] = jnp.dot(grad[...], w[n % 2], preferred_element_type=F32).astype(BF16)
+
+            @pl.when(n + 2 < units // TILE)
+            def _():
+                w_tile(n + 2).start()
+
+    def send_x(name, slot):
+        dy, dx = ORDER[slot]
+        (None, sets[name].near_right, sets[name].far, sets[name].near_left)[dx](dy)
+
+    def relay_x(name, slot):
+        dy, dx = ORDER[slot]
+        (None, sets[name].relay_right, None, sets[name].relay_left)[dx](dy)
+
+    scale = 1.0 / math.sqrt(tokens * 16)
+
+    def finish(name):
+        if name == "f":
+            factor[...] = fx.total() / (tokens * 16)
+        else:
+            wgrad[:, sets[name].cols] = (sets[name].total() * scale).astype(BF16)
+
+    gather_y(0)
+    gather_own(0)
+    act_there = send(own_act, act.at[pl.ds(tokens, tokens)], sibling)
+    for slot in range(1, CHIPS):
+        gather_y(slot)
     own_here.wait()
-    gather_z(0)
-    gather_z(1)
-    gather_sibling(0)
-    act_here.wait()
-    act_there.wait_recv()
-    for slot, (dy, dx) in enumerate(ORDER):
-        multiply(slot)
-        if dx == 2:
-            wx.far(dy)
-        if dx == 1:
-            wx.near_right(dy)
-        if dx == 3:
-            wx.near_left(dy)
-        if dy == 1:
-            wy.send_y(dx)
-        if slot + 2 < CHIPS:
-            gather_z(slot + 2)
-        if dx == 1:
-            wx.relay_right(dy)
-        if dx == 3:
-            wx.relay_left(dy)
-        if slot + 1 < CHIPS:
-            gather_sibling(slot + 1)
-        else:
-            cols = pl.ds(pl.multiple_of(t * chunk, chunk), chunk)
-            to_sibling["cols"] = send(grad.at[:, cols], grad_cols, sibling)
-        if dy == 0 and dx != 0:
-            wy.add_y(dx)
-            if dx == 2:
-                wy.far(0)
-            if dx == 1:
-                wy.near_right(0)
-                wy.relay_right(0)
-            if dx == 3:
-                wy.near_left(0)
-                wy.relay_left(0)
-
-    to_sibling["cols"].wait_recv()
-    for slot, (dy, dx) in enumerate(ORDER):
-        multiply_factor(slot)
-        if dx == 2:
-            fx.far(dy)
-        if dx == 1:
-            fx.near_right(dy)
-        if dx == 3:
-            fx.near_left(dy)
-    wx.end_y()
-    w_here.wait()
-    multiply_hidden(0, 2)
-    for dy in (1, 0):
-        fx.relay_right(dy)
-        fx.relay_left(dy)
-    multiply_hidden(2, 5)
-    fx.end_y()
-    multiply_hidden(5, units // TILE)
+    for n in range(2):
+        w_tile(n).start()
+    steps = {
+        "own": gather_own, "z": gather_z, "sib": gather_sibling, "cols": cols_z, "colsib": cols_sibling,
+        "mul": multiply, "fac": multiply_factor, "x": send_x, "relay": relay_x, "y": wy.send_y, "addy": wy.add_y,
+        "endy": lambda name: sets[name].end_y(), "hid": multiply_hidden, "fin": finish,
+    }
+    first = True
+    for name, *where in PLAN:
+        if name == "mul" and first:
+            act_here.wait()
+            act_there.wait_recv()
+            first = False
+        steps[name](*where)
     hidden_done = move(hidden, hidden_out)
-
-    scale = 1.0 / math.sqrt(tokens * 16)
-    wy.add_y(0)
-    wgrad[:, wx.cols] = (wx.total() * scale).astype(BF16)
-    wgrad[:, wy.cols] = (wy.total() * scale).astype(BF16)
     wgrad_done = move(wgrad, wgrad_out)
-    factor[...] = fx.total() / (tokens * 16)
     factor_done = move(factor, factor_out)
     for copy in remotes:
         copy.wait_send()
@@ -265,7 +285,7 @@
         return [relay, relay, end, end, over]
 
     def body(*refs):
-        kernel(*refs[:17], refs[17:32], *refs[32:])
+        kernel(*refs[:18], refs[18:33], *refs[33:])
 
     return pl.pallas_call(
         body,
@@ -280,8 +300,9 @@
             pltpu.VMEM((tokens, width), BF16),
             pltpu.VMEM((CHIPS, tokens, share), BF16),
             pltpu.VMEM((tokens, chunk), BF16),
+            pltpu.VMEM((tokens, chunk), BF16),
             pltpu.VMEM((2 * tokens, units), BF16),
-            pltpu.VMEM((width, units), BF16),
+            pltpu.VMEM((2, width, TILE), BF16),
             pltpu.VMEM((CHIPS, share, 2 * tokens), BF16),
             pltpu.VMEM((CHIPS, share, units), BF16),
             pltpu.VMEM((CHIPS, share, chunk), BF16),
@@ -294,9 +315,10 @@
             pltpu.SemaphoreType.DMA((COPIES,)),
             pltpu.SemaphoreType.DMA((COPIES,)),
             pltpu.SemaphoreType.DMA((8,)),
+            pltpu.SemaphoreType.DMA((2,)),
         ],
         compiler_params=pltpu.CompilerParams(
-            collective_id=0, has_side_effects=True, vmem_limit_bytes=60 * 2**20),
+            collective_id=0, has_side_effects=True, vmem_limit_bytes=50 * 2**20),
     )(out_grad, hidden_act, w_down)
 
 

time: 107 us -> 96.8 us (0.905); the launches traced: 105 us -> 96.6 us
  Pallas kernels: 99.1 us -> 92 us
  local copies, waits for them, and re-layouts: 5.09 us -> 3.98 us
    pallas_call x1, Pallas kernels: 99.1 us -> 92 us  [shards(): pl.pallas_call(body, out_shape=(jax.ShapeDtypeStruct((tokens, units), BF1...]
    unnamed x7 -> x5, local copies, waits for them, and re-layouts: 5.09 us -> 3.98 us
where the time goes in v2:
time: 96.8 us; the launch traced here: 96.6 us
  Pallas kernels  92 us (95%)
  local copies, waits for them, and re-layouts  3.98 us (4%)
    pallas_call x1, Pallas kernels, shards(): pl.pallas_call(body, out_shape=(jax.ShapeDtypeStruct((tokens, units), BF1...  92 us
    unnamed x5, local copies, waits for them, and re-layouts  3.98 us

profile of v2, /device:TPU:1, one launch (start us, length us, event | category | flops | bytes accessed | tf_op | source)
XLA Modules:
  0.0 96.6 jit_solution(12151522757126056569)
XLA Ops:
  0.6 0.0 copy-start
  0.6 1.0 %copy-done = bf16[64,4096]{1,0:T(8,128)(2,1)S(1)} copy-done((bf16[64,4096]{1,0:T(8,128)(2,1)S(1)}, bf16[64,4096]{1,0:T(8,128)(2,1)}, u32[]{:S(2)}) %copy-start) | copy-done | bytes 524312
  1.7 92.0 %shard_map.58 = (bf16[512,1792]{1,0:T(8,128)(2,1)S(1)}, bf16[256,1792]{1,0:T(8,128)(2,1)S(1)}, f32[256,512]{1,0:T(8,128)S(1)}) custom-call(bf16[64,4096]{1,0:T(8,128)(2,1)S(1)} %copy-done, bf16[512,1792]{1,0:T(8,128)(2,1)} %refs_1_.1, bf16[4096,1792]{1,0:T(8,128)(2,1)} %refs_2_.1), custom_call_target="tpu_custom_call" | custom-call | tf_op jit(solution)/shard_map/pallas_call | solution.py:290
  93.7 1.2 %copy.9 = bf16[512,1792]{1,0:T(8,128)(2,1)} copy(bf16[512,1792]{1,0:T(8,128)(2,1)S(1)} %get-tuple-element.6) | data formatting | bytes 3670016
  94.9 0.9 copy.10
  95.8 0.8 copy.11
Async XLA Ops:
  0.6 1.0 %copy-start = (bf16[64,4096]{1,0:T(8,128)(2,1)S(1)}, bf16[64,4096]{1,0:T(8,128)(2,1)}, u32[]{:S(2)}) copy-start(bf16[64,4096]{1,0:T(8,128)(2,1)} %refs_0_.1) | copy-start | bytes 1572868

commit v3 on v2

--- a/solution.py
+++ b/solution.py
@@ -11,26 +11,41 @@
 BF16 = jnp.bfloat16
 F32 = jnp.float32
 
-ORDER = ((1, 2), (0, 2), (1, 1), (1, 3), (0, 3), (0, 1), (1, 0), (0, 0))
+ORDER = ((1, 2), (0, 2), (1, 1), (0, 3), (1, 3), (0, 1), (1, 0), (0, 0))
 SLOT = {pair: slot for slot, pair in enumerate(ORDER)}
 CHIPS = len(ORDER)
 TILE = 256
-FIRST_X = 896
-COPIES = 128
+SETS = {
+    "wa": ("w", 0, 384, True),
+    "wb": ("w", 384, 384, True),
+    "va": ("w", 768, 512, False),
+    "vb": ("w", 1280, 512, False),
+    "f": ("f", 0, 512, True),
+}
+SPLIT = 768
+COPIES = 160
 
 
 EARLY = (0,)
+RELAYED = (1, 2, 3, 4, 5, 6, 7)
 PLAN = (
-    ("z", 0), ("z", 1), ("z", 2), ("z", 3), ("z", 4), ("sib", 0), ("mul", 0), ("x", "w", 0), ("y", 2), ("z", 5),
-    ("sib", 1), ("mul", 1), ("x", "w", 1), ("sib", 2), ("mul", 2), ("x", "w", 2), ("relay", "w", 2), ("y", 1),
-    ("z", 6), ("addy", 2), ("x", "v", 1), ("sib", 3), ("mul", 3), ("relay", "w", 3), ("y", 3), ("sib", 4), ("mul", 4),
-    ("relay", "w", 4), ("x", "w", 3), ("z", 7), ("cols",), ("sib", 5), ("mul", 5), ("addy", 1), ("relay", "v", 5),
-    ("relay", "w", 5), ("x", "w", 5), ("addy", 3), ("relay", "v", 4), ("x", "v", 4), ("sib", 7), ("sib", 6),
-    ("hid", 0, 1), ("mul", 6), ("y", 0), ("endy", "w"), ("colsib",), ("fac", 0), ("fac", 6), ("fac", 2), ("fac", 1),
-    ("x", "f", 0), ("fac", 5), ("fac", 4), ("x", "f", 5), ("fac", 3), ("x", "f", 3), ("relay", "f", 2),
-    ("relay", "f", 3), ("x", "f", 2), ("x", "f", 1), ("x", "f", 4), ("x", "w", 4), ("x", "v", 5), ("hid", 1, 5),
-    ("relay", "f", 4), ("endy", "f"), ("hid", 5, 7), ("relay", "f", 5), ("mul", 7), ("fac", 7), ("addy", 0),
-    ("fin", "v"), ("fin", "w"), ("fin", "f"),
+    ("z", 0), ("z", 1), ("z", 2), ("sib", 0), ("fwd", 1), ("z", 4), ("mul", 0), ("mulv", 0), ("y", "vb", 2),
+    ("y", "va", 2), ("fwd", 2), ("z", 3), ("x", "wa", 0), ("sib", 1), ("x", "wb", 0), ("mul", 1), ("fwd", 4),
+    ("z", 6), ("x", "wb", 1), ("sib", 2), ("z", 5), ("x", "wa", 1), ("mulv", 1), ("mul", 2), ("x", "wb", 2),
+    ("x", "wa", 2), ("addy", "vb", 2), ("x", "vb", 1), ("sib", 4), ("fwd", 3), ("mulv", 2), ("y", "va", 1),
+    ("mul", 4), ("x", "wa", 4), ("fwd", 6), ("relay", "wb", 4), ("mulv", 4), ("y", "vb", 3), ("x", "wb", 4),
+    ("fwd", 5), ("addy", "va", 2), ("z", 7), ("cols",), ("relay", "wb", 2), ("relay", "wa", 2), ("sib", 3),
+    ("relay", "wa", 4), ("sib", 6), ("y", "vb", 1), ("x", "va", 1), ("sib", 5), ("mul", 3), ("mulv", 3),
+    ("x", "wa", 3), ("mul", 5), ("x", "wb", 5), ("relay", "wa", 3), ("relay", "wb", 3), ("relay", "wa", 5),
+    ("fwd", 7), ("mul", 6), ("endy", "wb"), ("relay", "wb", 5), ("endy", "wa"), ("colsib",), ("addy", "vb", 3),
+    ("x", "vb", 3), ("x", "wa", 5), ("mulv", 5), ("addy", "va", 1), ("fac", 0), ("x", "f", 0), ("fac", 2),
+    ("x", "f", 2), ("sib", 7), ("fac", 3), ("addy", "vb", 1), ("fac", 4), ("x", "f", 3), ("fac", 6), ("y", "va", 3),
+    ("x", "vb", 5), ("mulv", 6), ("fac", 1), ("x", "f", 1), ("y", "vb", 0), ("x", "f", 4), ("mul", 7),
+    ("relay", "f", 2), ("y", "va", 0), ("x", "wb", 3), ("hid", 0, 1), ("relay", "f", 4), ("relay", "va", 5),
+    ("fac", 5), ("x", "f", 5), ("relay", "vb", 5), ("relay", "vb", 3), ("hid", 1, 3), ("addy", "va", 3),
+    ("x", "va", 3), ("relay", "va", 3), ("x", "va", 5), ("relay", "f", 3), ("hid", 3, 5), ("fin", "wb"),
+    ("endy", "f"), ("hid", 5, 7), ("relay", "f", 5), ("mulv", 7), ("addy", "vb", 0), ("fin", "vb"), ("addy", "va", 0),
+    ("fin", "va"), ("fin", "wa"), ("fac", 7), ("fin", "f"),
 )
 
 
@@ -57,13 +72,14 @@
     across = ((1 - y) * 8 + x * 2 + core, t)
     partner = (dp, z * 2 + 1 - y_lo)
     along = (2, 1, 3)
+    up, down = on_z(1), on_z(3)
 
     barrier = pltpu.get_barrier_semaphore()
     everyone = (sibling, right, left_chip, across, partner) + tuple(on_z(step) for step in along)
     for device in everyone:
         pl.semaphore_signal(barrier, inc=1, device_id=device, device_id_type=MESH)
 
-    remotes, locals_ = [], []
+    remotes, locals_, results = [], [], []
 
     def send(src, dst, device):
         number = len(remotes)
@@ -118,7 +134,17 @@
     def gather_z(slot):
         from_partner[slot].wait_recv()
         piece = grad.at[partner_rows if slot in EARLY else pair_rows, columns(slot)]
-        along_z.setdefault(slot, []).extend([send(piece, piece, on_z(step)) for step in along])
+        steps = (1, 3) if slot in RELAYED else along
+        along_z.setdefault(slot, []).extend([send(piece, piece, on_z(step)) for step in steps])
+
+    def forward_z(slot):
+        copies = []
+        for copy, step, low, device in zip(along_z[slot], (3, 1), (0, rows), (up, down)):
+            copy.wait_recv()
+            first = ((z + step) % 4) * 2 * rows + low
+            piece = grad.at[pl.ds(pl.multiple_of(first, rows), rows), columns(slot)]
+            copies.append(send(piece, piece, device))
+        along_z[slot] = copies
 
     def gather_sibling(slot):
         for copy in along_z[slot]:
@@ -193,21 +219,31 @@
                 value = value + self.box_y[...].astype(F32)
             return value
 
-    wx = Columns(part_w, 0, FIRST_X, True, boxes[0:5])
-    wy = Columns(part_w, FIRST_X, units - FIRST_X, False, boxes[5:10])
-    fx = Columns(part_f, 0, chunk, True, boxes[10:15])
-
-    sets = {"w": wx, "v": wy, "f": fx}
+    sets, parts = {}, {"w": part_w, "f": part_f}
+    for number, (name, (part, start, count, x_first)) in enumerate(SETS.items()):
+        sets[name] = Columns(parts[part], start, count, x_first, boxes[5 * number:5 * number + 5])
 
     def multiply(slot):
         to_sibling[slot].wait_recv()
         left[slot, :, pl.ds(0, tokens)] = grad[:, share_of(slot, core)].T
         left[slot, :, pl.ds(tokens, tokens)] = grad_sib[slot].T
-
-        @pl.loop(0, units // TILE)
+        multiply_cols(slot, 0, SPLIT)
+
+    def multiply_rest(slot):
+        multiply_cols(slot, SPLIT, units)
+
+    def multiply_cols(slot, start, end):
+        def product(tile):
+            part_w[slot, :, tile] = jnp.dot(left[slot], act[:, tile], preferred_element_type=F32).astype(BF16)
+
+        full = (end - start) // TILE
+
+        @pl.loop(0, full)
         def _(n):
-            tile = pl.ds(pl.multiple_of(n * TILE, TILE), TILE)
-            part_w[slot, :, tile] = jnp.dot(left[slot], act[:, tile], preferred_element_type=F32).astype(BF16)
+            product(pl.ds(pl.multiple_of(start + n * TILE, TILE // 2), TILE))
+
+        if start + full * TILE < end:
+            product(pl.ds(start + full * TILE, end - start - full * TILE))
 
     def multiply_factor(slot):
         if slot == 0:
@@ -227,6 +263,9 @@
             def _():
                 w_tile(n + 2).start()
 
+        if last == units // TILE:
+            results.append(move(hidden, hidden_out))
+
     def send_x(name, slot):
         dy, dx = ORDER[slot]
         (None, sets[name].near_right, sets[name].far, sets[name].near_left)[dx](dy)
@@ -238,10 +277,12 @@
     scale = 1.0 / math.sqrt(tokens * 16)
 
     def finish(name):
-        if name == "f":
-            factor[...] = fx.total() / (tokens * 16)
+        if SETS[name][0] == "f":
+            factor[:, sets[name].cols] = sets[name].total() / (tokens * 16)
+            results.append(move(factor.at[:, sets[name].cols], factor_out.at[:, sets[name].cols]))
         else:
             wgrad[:, sets[name].cols] = (sets[name].total() * scale).astype(BF16)
+            results.append(move(wgrad.at[:, sets[name].cols], wgrad_out.at[:, sets[name].cols]))
 
     gather_y(0)
     gather_own(0)
@@ -253,7 +294,8 @@
         w_tile(n).start()
     steps = {
         "own": gather_own, "z": gather_z, "sib": gather_sibling, "cols": cols_z, "colsib": cols_sibling,
-        "mul": multiply, "fac": multiply_factor, "x": send_x, "relay": relay_x, "y": wy.send_y, "addy": wy.add_y,
+        "fwd": forward_z, "mul": multiply, "mulv": multiply_rest, "fac": multiply_factor, "x": send_x, "relay": relay_x,
+        "y": lambda name, dx: sets[name].send_y(dx), "addy": lambda name, dx: sets[name].add_y(dx),
         "endy": lambda name: sets[name].end_y(), "hid": multiply_hidden, "fin": finish,
     }
     first = True
@@ -263,12 +305,9 @@
             act_there.wait_recv()
             first = False
         steps[name](*where)
-    hidden_done = move(hidden, hidden_out)
-    wgrad_done = move(wgrad, wgrad_out)
-    factor_done = move(factor, factor_out)
     for copy in remotes:
         copy.wait_send()
-    for copy in (hidden_done, wgrad_done, factor_done):
+    for copy in results:
         copy.wait()
 
 
@@ -285,9 +324,9 @@
         return [relay, relay, end, end, over]
 
     def body(*refs):
-        kernel(*refs[:18], refs[18:33], *refs[33:])
-
-    return pl.pallas_call(
+        kernel(*refs[:18], refs[18:-4], *refs[-4:])
+
+    return publish(*pl.pallas_call(
         body,
         out_shape=(
             jax.ShapeDtypeStruct((tokens, units), BF16),
@@ -309,17 +348,34 @@
             pltpu.VMEM((tokens, units), BF16),
             pltpu.VMEM((share, units), BF16),
             pltpu.VMEM((share, chunk), F32),
-            *boxes(FIRST_X, True),
-            *boxes(units - FIRST_X, False),
-            *boxes(chunk, True),
+            *[box for _, _, count, x_first in SETS.values() for box in boxes(count, x_first)],
             pltpu.SemaphoreType.DMA((COPIES,)),
             pltpu.SemaphoreType.DMA((COPIES,)),
-            pltpu.SemaphoreType.DMA((8,)),
+            pltpu.SemaphoreType.DMA((16,)),
             pltpu.SemaphoreType.DMA((2,)),
         ],
         compiler_params=pltpu.CompilerParams(
             collective_id=0, has_side_effects=True, vmem_limit_bytes=50 * 2**20),
-    )(out_grad, hidden_act, w_down)
+    )(out_grad, hidden_act, w_down))
+
+
+def publish(hidden, wgrad, factor):
+    def body(*refs):
+        sems = refs[6]
+        copies = [pltpu.make_async_copy(refs[i], refs[3 + i], sems.at[i]) for i in range(3)]
+        for copy in copies:
+            copy.start()
+        for copy in copies:
+            copy.wait()
+
+    return pl.pallas_call(
+        body,
+        out_shape=tuple(jax.ShapeDtypeStruct(a.shape, a.dtype) for a in (hidden, wgrad, factor)),
+        in_specs=[pl.BlockSpec(memory_space=pl.ANY)] * 3,
+        out_specs=(pl.BlockSpec(memory_space=pl.ANY),) * 3,
+        scratch_shapes=[pltpu.SemaphoreType.DMA((3,))],
+        compiler_params=pltpu.CompilerParams(vmem_limit_bytes=2**20),
+    )(hidden, wgrad, factor)
 
 
 def solution(mesh):

time: 96.8 us -> 90.2 us (0.932)
  Pallas kernels: 92 us -> 88.4 us
  local copies, waits for them, and re-layouts: 3.98 us -> 1.03 us
    pallas_call x1, Pallas kernels: 92 us -> 86.7 us  [shards(): pl.pallas_call(body, out_shape=(jax.ShapeDtypeStruct((tokens, units), BF1...]
    unnamed x5 -> x2, local copies, waits for them, and re-layouts: 3.98 us -> 1.03 us
    pallas_call x0 -> x1, Pallas kernels: none -> 1.73 us  [publish(): pl.pallas_call(body, out_shape=tuple((jax.ShapeDtypeStruct(a.shape, a.dty...]
where the time goes in v3:
time: 90.2 us; the launch traced here: 90.1 us
  Pallas kernels  88.4 us (98%)
  local copies, waits for them, and re-layouts  1.03 us (1%)
    pallas_call x1, Pallas kernels, shards(): pl.pallas_call(body, out_shape=(jax.ShapeDtypeStruct((tokens, units), BF1...  86.7 us

profile of v3, /device:TPU:1, one launch (start us, length us, event | category | flops | bytes accessed | tf_op | source)
XLA Modules:
  0.0 90.1 jit_solution(15412629718537892602)
XLA Ops:
  0.6 0.0 copy-start
  0.6 1.0 %copy-done = bf16[64,4096]{1,0:T(8,128)(2,1)S(1)} copy-done((bf16[64,4096]{1,0:T(8,128)(2,1)S(1)}, bf16[64,4096]{1,0:T(8,128)(2,1)}, u32[]{:S(2)}) %copy-start) | copy-done | bytes 524312
  1.7 86.7 %shard_map.58 = (bf16[512,1792]{1,0:T(8,128)(2,1)S(1)}, bf16[256,1792]{1,0:T(8,128)(2,1)S(1)}, f32[256,512]{1,0:T(8,128)S(1)}) custom-call(bf16[64,4096]{1,0:T(8,128)(2,1)S(1)} %copy-done, bf16[512,1792]{1,0:T(8,128)(2,1)} %refs_1_.1, bf16[4096,1792]{1,0:T(8,128)(2,1)} %refs_2_.1), custom_call_target="tpu_custom_call" | custom-call | tf_op jit(solution)/shard_map/pallas_call | solution.py:329
  88.4 1.7 %shard_map.59 = (bf16[512,1792]{1,0:T(8,128)(2,1)}, bf16[256,1792]{1,0:T(8,128)(2,1)}, f32[256,512]{1,0:T(8,128)}) custom-call(bf16[512,1792]{1,0:T(8,128)(2,1)S(1)} %get-tuple-element.6.refs_0_, bf16[256,1792]{1,0:T(8,128)(2,1)S(1)} %get-tuple-element.7.refs_1_, f32[256,512]{1,0:T(8,128)S(1)} %get-tuple-element.8.refs_2_), custom_call_target="tpu_custom_call" | custom-call | tf_op jit(solution)/shard_map/pallas_call | solution.py:371
Async XLA Ops:
  0.6 1.0 %copy-start = (bf16[64,4096]{1,0:T(8,128)(2,1)S(1)}, bf16[64,4096]{1,0:T(8,128)(2,1)}, u32[]{:S(2)}) copy-start(bf16[64,4096]{1,0:T(8,128)(2,1)} %refs_0_.1) | copy-start | bytes 1572868

commit v4 on v3

--- a/solution.py
+++ b/solution.py
@@ -11,16 +11,17 @@
 BF16 = jnp.bfloat16
 F32 = jnp.float32
 
-ORDER = ((1, 2), (0, 2), (1, 1), (0, 3), (1, 3), (0, 1), (1, 0), (0, 0))
+ORDER = ((1, 2), (0, 2), (1, 1), (1, 3), (1, 0), (0, 3), (0, 1), (0, 0))
 SLOT = {pair: slot for slot, pair in enumerate(ORDER)}
 CHIPS = len(ORDER)
 TILE = 256
 SETS = {
-    "wa": ("w", 0, 384, True),
-    "wb": ("w", 384, 384, True),
+    "wa": ("w", 0, 256, True),
+    "wb": ("w", 256, 512, True),
     "va": ("w", 768, 512, False),
-    "vb": ("w", 1280, 512, False),
-    "f": ("f", 0, 512, True),
+    "vb": ("w", 1280, 256, False),
+    "vc": ("w", 1536, 256, False),
+    "fa": ("f", 0, 512, True),
 }
 SPLIT = 768
 COPIES = 160
@@ -29,23 +30,26 @@
 EARLY = (0,)
 RELAYED = (1, 2, 3, 4, 5, 6, 7)
 PLAN = (
-    ("z", 0), ("z", 1), ("z", 2), ("sib", 0), ("fwd", 1), ("z", 4), ("mul", 0), ("mulv", 0), ("y", "vb", 2),
-    ("y", "va", 2), ("fwd", 2), ("z", 3), ("x", "wa", 0), ("sib", 1), ("x", "wb", 0), ("mul", 1), ("fwd", 4),
-    ("z", 6), ("x", "wb", 1), ("sib", 2), ("z", 5), ("x", "wa", 1), ("mulv", 1), ("mul", 2), ("x", "wb", 2),
-    ("x", "wa", 2), ("addy", "vb", 2), ("x", "vb", 1), ("sib", 4), ("fwd", 3), ("mulv", 2), ("y", "va", 1),
-    ("mul", 4), ("x", "wa", 4), ("fwd", 6), ("relay", "wb", 4), ("mulv", 4), ("y", "vb", 3), ("x", "wb", 4),
-    ("fwd", 5), ("addy", "va", 2), ("z", 7), ("cols",), ("relay", "wb", 2), ("relay", "wa", 2), ("sib", 3),
-    ("relay", "wa", 4), ("sib", 6), ("y", "vb", 1), ("x", "va", 1), ("sib", 5), ("mul", 3), ("mulv", 3),
-    ("x", "wa", 3), ("mul", 5), ("x", "wb", 5), ("relay", "wa", 3), ("relay", "wb", 3), ("relay", "wa", 5),
-    ("fwd", 7), ("mul", 6), ("endy", "wb"), ("relay", "wb", 5), ("endy", "wa"), ("colsib",), ("addy", "vb", 3),
-    ("x", "vb", 3), ("x", "wa", 5), ("mulv", 5), ("addy", "va", 1), ("fac", 0), ("x", "f", 0), ("fac", 2),
-    ("x", "f", 2), ("sib", 7), ("fac", 3), ("addy", "vb", 1), ("fac", 4), ("x", "f", 3), ("fac", 6), ("y", "va", 3),
-    ("x", "vb", 5), ("mulv", 6), ("fac", 1), ("x", "f", 1), ("y", "vb", 0), ("x", "f", 4), ("mul", 7),
-    ("relay", "f", 2), ("y", "va", 0), ("x", "wb", 3), ("hid", 0, 1), ("relay", "f", 4), ("relay", "va", 5),
-    ("fac", 5), ("x", "f", 5), ("relay", "vb", 5), ("relay", "vb", 3), ("hid", 1, 3), ("addy", "va", 3),
-    ("x", "va", 3), ("relay", "va", 3), ("x", "va", 5), ("relay", "f", 3), ("hid", 3, 5), ("fin", "wb"),
-    ("endy", "f"), ("hid", 5, 7), ("relay", "f", 5), ("mulv", 7), ("addy", "vb", 0), ("fin", "vb"), ("addy", "va", 0),
-    ("fin", "va"), ("fin", "wa"), ("fac", 7), ("fin", "f"),
+    ("yw", 0), ("z", 0), ("yw", 1), ("z", 1), ("yw", 3), ("yw", 2), ("z", 2), ("sib", 0), ("fwd", 1), ("z", 3),
+    ("mul", 0), ("mulv", 0), ("y", "va", 2), ("x", "wa", 0), ("fwd", 2), ("sib", 1), ("yw", 6), ("z", 6),
+    ("x", "wb", 0), ("y", "vc", 2), ("yw", 5), ("mul", 1), ("x", "wb", 1), ("y", "vb", 2), ("fwd", 3), ("sib", 2),
+    ("z", 5), ("mulv", 1), ("x", "wa", 1), ("mul", 2), ("addy", "va", 2), ("x", "va", 1), ("yw", 4), ("z", 4),
+    ("sib", 3), ("mulv", 2), ("y", "vb", 1), ("y", "vc", 1), ("relay", "wb", 2), ("fwd", 6), ("addy", "vc", 2),
+    ("x", "vc", 1), ("mul", 3), ("x", "wb", 3), ("x", "wa", 2), ("relay", "wa", 2), ("relay", "wb", 3), ("fwd", 5),
+    ("mulv", 3), ("y", "vc", 3), ("relay", "wa", 3), ("addy", "vb", 2), ("fwd", 4), ("x", "wb", 2), ("yw", 7),
+    ("cols",), ("x", "vb", 1), ("sib", 6), ("y", "vb", 3), ("sib", 5), ("mul", 6), ("x", "wb", 6), ("x", "wa", 6),
+    ("sib", 4), ("y", "va", 3), ("x", "wa", 3), ("z", 7), ("mul", 5), ("relay", "wa", 5), ("mulv", 5), ("mul", 4),
+    ("x", "wb", 5), ("relay", "wb", 6), ("mulv", 6), ("x", "wa", 5), ("addy", "vc", 1), ("colsib",), ("endy", "wb"),
+    ("addy", "vb", 3), ("relay", "vc", 6), ("x", "vb", 5), ("addy", "vc", 3), ("y", "va", 1), ("mulv", 4),
+    ("relay", "wb", 5), ("y", "vb", 0), ("fwd", 7), ("fac", 0), ("x", "fa", 0), ("fac", 1), ("x", "fa", 1),
+    ("relay", "vc", 5), ("addy", "vb", 1), ("x", "vb", 6), ("relay", "vb", 6), ("x", "vc", 5), ("fac", 2),
+    ("x", "fa", 2), ("x", "vc", 6), ("y", "vc", 0), ("fac", 3), ("x", "fa", 3), ("relay", "wa", 6), ("endy", "wa"),
+    ("relay", "vb", 5), ("sib", 7), ("hid", 0, 3), ("y", "va", 0), ("relay", "fa", 3), ("addy", "va", 3),
+    ("hid", 3, 4), ("relay", "fa", 2), ("hid", 4, 5), ("addy", "va", 1), ("x", "va", 6), ("x", "va", 5),
+    ("relay", "va", 6), ("mul", 7), ("fac", 7), ("mulv", 7), ("addy", "vb", 0), ("fin", "vb"), ("fac", 5),
+    ("relay", "va", 5), ("relay", "fa", 5), ("fac", 4), ("endy", "fa"), ("addy", "vc", 0), ("fac", 6), ("x", "fa", 6),
+    ("relay", "fa", 6), ("fin", "vc"), ("fin", "wa"), ("x", "fa", 5), ("fin", "wb"), ("hid", 5, 7), ("addy", "va", 0),
+    ("fin", "va"), ("fin", "fa"),
 )
 
 
@@ -131,8 +135,10 @@
         piece = columns(slot)
         along_z[slot] = [send(own_grad.at[:, piece], grad.at[own_rows, piece], on_z(step)) for step in along]
 
+    def wait_y(slot):
+        from_partner[slot].wait_recv()
+
     def gather_z(slot):
-        from_partner[slot].wait_recv()
         piece = grad.at[partner_rows if slot in EARLY else pair_rows, columns(slot)]
         steps = (1, 3) if slot in RELAYED else along
         along_z.setdefault(slot, []).extend([send(piece, piece, on_z(step)) for step in steps])
@@ -293,19 +299,25 @@
     for n in range(2):
         w_tile(n).start()
     steps = {
-        "own": gather_own, "z": gather_z, "sib": gather_sibling, "cols": cols_z, "colsib": cols_sibling,
+        "yw": wait_y, "own": gather_own, "z": gather_z, "sib": gather_sibling, "cols": cols_z, "colsib": cols_sibling,
         "fwd": forward_z, "mul": multiply, "mulv": multiply_rest, "fac": multiply_factor, "x": send_x, "relay": relay_x,
         "y": lambda name, dx: sets[name].send_y(dx), "addy": lambda name, dx: sets[name].add_y(dx),
         "endy": lambda name: sets[name].end_y(), "hid": multiply_hidden, "fin": finish,
     }
     first = True
-    for name, *where in PLAN:
+    drained = 0
+    for step, (name, *where) in enumerate(PLAN):
         if name == "mul" and first:
             act_here.wait()
             act_there.wait_recv()
             first = False
         steps[name](*where)
-    for copy in remotes:
+        if name in ("hid", "endy", "fin") and step > len(PLAN) // 2:
+            upto = max(drained, len(remotes) - 20)
+            for copy in remotes[drained:upto]:
+                copy.wait_send()
+            drained = upto
+    for copy in remotes[drained:]:
         copy.wait_send()
     for copy in results:
         copy.wait()

time: 90.2 us -> 89.6 us (level)
  no operation moved by 1% of the time
where the time goes in v4:
time: 89.6 us; the launch traced here: 89.5 us
  Pallas kernels  87.8 us (98%)
  local copies, waits for them, and re-layouts  1.03 us (1%)
    pallas_call x1, Pallas kernels, shards(): pl.pallas_call(body, out_shape=(jax.ShapeDtypeStruct((tokens, units), BF1...  86.1 us

profile of v4, /device:TPU:1, one launch (start us, length us, event | category | flops | bytes accessed | tf_op | source)
XLA Modules:
  0.0 89.5 jit_solution(18275264116180619133)
XLA Ops:
  0.6 0.0 copy-start
  0.6 1.0 %copy-done = bf16[64,4096]{1,0:T(8,128)(2,1)S(1)} copy-done((bf16[64,4096]{1,0:T(8,128)(2,1)S(1)}, bf16[64,4096]{1,0:T(8,128)(2,1)}, u32[]{:S(2)}) %copy-start) | copy-done | bytes 524312
  1.7 86.1 %shard_map.58 = (bf16[512,1792]{1,0:T(8,128)(2,1)S(1)}, bf16[256,1792]{1,0:T(8,128)(2,1)S(1)}, f32[256,512]{1,0:T(8,128)S(1)}) custom-call(bf16[64,4096]{1,0:T(8,128)(2,1)S(1)} %copy-done, bf16[512,1792]{1,0:T(8,128)(2,1)} %refs_1_.1, bf16[4096,1792]{1,0:T(8,128)(2,1)} %refs_2_.1), custom_call_target="tpu_custom_call" | custom-call | tf_op jit(solution)/shard_map/pallas_call | solution.py:341
  87.7 1.7 %shard_map.59 = (bf16[512,1792]{1,0:T(8,128)(2,1)}, bf16[256,1792]{1,0:T(8,128)(2,1)}, f32[256,512]{1,0:T(8,128)}) custom-call(bf16[512,1792]{1,0:T(8,128)(2,1)S(1)} %get-tuple-element.6.refs_0_, bf16[256,1792]{1,0:T(8,128)(2,1)S(1)} %get-tuple-element.7.refs_1_, f32[256,512]{1,0:T(8,128)S(1)} %get-tuple-element.8.refs_2_), custom_call_target="tpu_custom_call" | custom-call | tf_op jit(solution)/shard_map/pallas_call | solution.py:383
Async XLA Ops:
  0.6 1.0 %copy-start = (bf16[64,4096]{1,0:T(8,128)(2,1)S(1)}, bf16[64,4096]{1,0:T(8,128)(2,1)}, u32[]{:S(2)}) copy-start(bf16[64,4096]{1,0:T(8,128)(2,1)} %refs_0_.1) | copy-start | bytes 1572868

commit v5 on v4

--- a/solution.py
+++ b/solution.py
@@ -24,6 +24,7 @@
     "fa": ("f", 0, 512, True),
 }
 SPLIT = 768
+FIRST_SENT = 256
 COPIES = 160
 
 
@@ -31,8 +32,9 @@
 RELAYED = (1, 2, 3, 4, 5, 6, 7)
 PLAN = (
     ("yw", 0), ("z", 0), ("yw", 1), ("z", 1), ("yw", 3), ("yw", 2), ("z", 2), ("sib", 0), ("fwd", 1), ("z", 3),
-    ("mul", 0), ("mulv", 0), ("y", "va", 2), ("x", "wa", 0), ("fwd", 2), ("sib", 1), ("yw", 6), ("z", 6),
-    ("x", "wb", 0), ("y", "vc", 2), ("yw", 5), ("mul", 1), ("x", "wb", 1), ("y", "vb", 2), ("fwd", 3), ("sib", 2),
+    ("mul", 0), ("x", "wa", 0), ("mulb", 0),
+    ("x", "wb", 0), ("mulv", 0), ("y", "va", 2), ("fwd", 2), ("sib", 1), ("yw", 6), ("z", 6),
+    ("y", "vc", 2), ("yw", 5), ("mul", 1), ("x", "wb", 1), ("y", "vb", 2), ("fwd", 3), ("sib", 2),
     ("z", 5), ("mulv", 1), ("x", "wa", 1), ("mul", 2), ("addy", "va", 2), ("x", "va", 1), ("yw", 4), ("z", 4),
     ("sib", 3), ("mulv", 2), ("y", "vb", 1), ("y", "vc", 1), ("relay", "wb", 2), ("fwd", 6), ("addy", "vc", 2),
     ("x", "vc", 1), ("mul", 3), ("x", "wb", 3), ("x", "wa", 2), ("relay", "wa", 2), ("relay", "wb", 3), ("fwd", 5),
@@ -233,7 +235,10 @@
         to_sibling[slot].wait_recv()
         left[slot, :, pl.ds(0, tokens)] = grad[:, share_of(slot, core)].T
         left[slot, :, pl.ds(tokens, tokens)] = grad_sib[slot].T
-        multiply_cols(slot, 0, SPLIT)
+        multiply_cols(slot, 0, FIRST_SENT if slot == 0 else SPLIT)
+
+    def multiply_second(slot):
+        multiply_cols(slot, FIRST_SENT, SPLIT)
 
     def multiply_rest(slot):
         multiply_cols(slot, SPLIT, units)
@@ -300,7 +305,7 @@
         w_tile(n).start()
     steps = {
         "yw": wait_y, "own": gather_own, "z": gather_z, "sib": gather_sibling, "cols": cols_z, "colsib": cols_sibling,
-        "fwd": forward_z, "mul": multiply, "mulv": multiply_rest, "fac": multiply_factor, "x": send_x, "relay": relay_x,
+        "fwd": forward_z, "mul": multiply, "mulb": multiply_second, "mulv": multiply_rest, "fac": multiply_factor, "x": send_x, "relay": relay_x,
         "y": lambda name, dx: sets[name].send_y(dx), "addy": lambda name, dx: sets[name].add_y(dx),
         "endy": lambda name: sets[name].end_y(), "hid": multiply_hidden, "fin": finish,
     }

time: 89.6 us -> 89.8 us (level)
  no operation moved by 1% of the time
where the time goes in v5:
time: 89.8 us; the launch traced here: 89.6 us
  Pallas kernels  88 us (98%)
  local copies, waits for them, and re-layouts  1.03 us (1%)
    pallas_call x1, Pallas kernels, shards(): pl.pallas_call(body, out_shape=(jax.ShapeDtypeStruct((tokens, units), BF1...  86.2 us

profile of v5, /device:TPU:1, one launch (start us, length us, event | category | flops | bytes accessed | tf_op | source)
XLA Modules:
  0.0 89.6 jit_solution(5846849982249221117)
XLA Ops:
  0.6 0.0 copy-start
  0.6 1.0 %copy-done = bf16[64,4096]{1,0:T(8,128)(2,1)S(1)} copy-done((bf16[64,4096]{1,0:T(8,128)(2,1)S(1)}, bf16[64,4096]{1,0:T(8,128)(2,1)}, u32[]{:S(2)}) %copy-start) | copy-done | bytes 524312
  1.7 86.2 %shard_map.58 = (bf16[512,1792]{1,0:T(8,128)(2,1)S(1)}, bf16[256,1792]{1,0:T(8,128)(2,1)S(1)}, f32[256,512]{1,0:T(8,128)S(1)}) custom-call(bf16[64,4096]{1,0:T(8,128)(2,1)S(1)} %copy-done, bf16[512,1792]{1,0:T(8,128)(2,1)} %refs_1_.1, bf16[4096,1792]{1,0:T(8,128)(2,1)} %refs_2_.1), custom_call_target="tpu_custom_call" | custom-call | tf_op jit(solution)/shard_map/pallas_call | solution.py:346
  87.9 1.7 %shard_map.59 = (bf16[512,1792]{1,0:T(8,128)(2,1)}, bf16[256,1792]{1,0:T(8,128)(2,1)}, f32[256,512]{1,0:T(8,128)}) custom-call(bf16[512,1792]{1,0:T(8,128)(2,1)S(1)} %get-tuple-element.6.refs_0_, bf16[256,1792]{1,0:T(8,128)(2,1)S(1)} %get-tuple-element.7.refs_1_, f32[256,512]{1,0:T(8,128)S(1)} %get-tuple-element.8.refs_2_), custom_call_target="tpu_custom_call" | custom-call | tf_op jit(solution)/shard_map/pallas_call | solution.py:388
Async XLA Ops:
  0.6 1.0 %copy-start = (bf16[64,4096]{1,0:T(8,128)(2,1)S(1)}, bf16[64,4096]{1,0:T(8,128)(2,1)}, u32[]{:S(2)}) copy-start(bf16[64,4096]{1,0:T(8,128)(2,1)} %refs_0_.1) | copy-start | bytes 1572868
